TPU v7x, 256 devices: a whole 4x4x8 slice. The times are simulated.
256 devices in a mesh: row: 8 (over x, core), col: 8 (over z_hi, y), depth: 4 (over z_lo).
Axes of the slice: x: 4, y: 4, z: 8 (z_hi: 2, z_lo: 4; z = z_hi * 4 + z_lo), core: 2. Of those that a mesh axis runs over, the one named last changes fastest.
Arguments:
- amplitudes: bfloat16 [6400, 60000], P('row', ('col', 'depth')), may hold values from -6 to 6
- integrals: bfloat16 [60000, 2400], P(('col', 'depth'), 'row'), may hold values from -0.125 to 0.125
- virtual_irrep: int32 [600], replicated, may hold values from 0 to 7
- occupied_irrep: int32 [100], replicated, may hold values from 0 to 7
- row_start: int32 [1], replicated, may hold values from 0 to 536
- column_start: int32 [1], replicated, may hold values from 0 to 576
Outputs:
- cycle: bfloat16 [2400, 6400], P(('col', 'depth'), 'row')
All inputs are finite; a program needn't handle non-finite values.
Results may differ from a plain program's by a relative error of at most 0.001.
Values may be sent and summed in bfloat16 or wider, within the bound.
No kernel may reach another device: no remote copies, remote signals or barrier semaphores. Data moves between devices by JAX's collectives and lax.ppermute only.
A program may use at most 64 MiB of HBM per device.

v0:
```python
import jax
import jax.numpy as jnp
from jax import lax
from jax.sharding import PartitionSpec as P

VA = 64
VB = 24


def pair_labels(virtual_part, occupied_irrep):
    return jnp.bitwise_xor(virtual_part[:, None], occupied_irrep[None, :]).reshape(-1)


def cycle_rows(columns, masked_amplitudes):
    return lax.dot_general(
        columns, masked_amplitudes, (((0,), (1,)), ((), ())), preferred_element_type=jnp.float32
    )


def body(amplitudes, integrals, virtual_irrep, occupied_irrep, row_start, column_start):
    local_rows, block_pairs = amplitudes.shape
    local_columns = integrals.shape[1]
    pair_block = lax.axis_index(("col", "depth"))
    row_block = lax.axis_index("row")
    row_label = pair_labels(
        lax.dynamic_slice_in_dim(virtual_irrep, row_start[0], VA), occupied_irrep
    )
    column_label = pair_labels(
        lax.dynamic_slice_in_dim(virtual_irrep, column_start[0], VB), occupied_irrep
    )
    pair_label = pair_labels(virtual_irrep, occupied_irrep)
    pair_here = lax.dynamic_slice_in_dim(pair_label, pair_block * block_pairs, block_pairs)
    row_here = lax.dynamic_slice_in_dim(row_label, row_block * local_rows, local_rows)
    column_here = lax.dynamic_slice_in_dim(column_label, row_block * local_columns, local_columns)
    masked_amplitudes = jnp.where(
        row_here[:, None] == pair_here[None, :], amplitudes, jnp.zeros_like(amplitudes)
    )
    masked_integrals = jnp.where(
        pair_here[:, None] == column_here[None, :], integrals, jnp.zeros_like(integrals)
    )
    whole_columns = lax.all_gather(masked_integrals, "row", axis=1, tiled=True)
    summed = lax.psum_scatter(
        cycle_rows(whole_columns, masked_amplitudes),
        ("col", "depth"),
        scatter_dimension=0,
        tiled=True,
    )
    return summed.astype(jnp.bfloat16)


def solution(mesh):
    return jax.shard_map(
        body,
        mesh=mesh,
        in_specs=(P("row", ("col", "depth")), P(("col", "depth"), "row"), P(), P(), P(), P()),
        out_specs=P(("col", "depth"), "row"),
        check_vma=False,
    )
```

profile of v0, /device:TPU:8, one launch (start us, length us, event | category | flops | bytes accessed | tf_op | source)
XLA Modules:
  0.0 322.7 jit_solution(16809652381148259718)
XLA Ops:
  6.5 0.0 copy-start
  6.5 0.0 all-gather.3.cloned.1.call-start
  7.2 0.8 dynamic_slice.16
  8.0 0.8 broadcast_xor_fusion
  8.8 0.7 broadcast_xor_fusion.2
  9.6 0.1 xor.58
  9.7 0.3 xor.54
  10.0 0.1 dynamic_slice.17
  10.1 0.1 dynamic_slice.15
  10.2 2.7 fusion.5
  12.8 0.0 all-gather.3.cloned.1.call-update
  13.5 0.8 dynamic_slice.18
  14.3 0.0 copy-done
  14.3 0.1 broadcast_xor_fusion.1
  14.3 0.1 xor.62
  14.5 0.1 dynamic_slice.19
  14.5 0.0 copy-start.2
  14.5 57.6 %all-gather.3.cloned.1.call-done = bf16[8,300,1875]{2,1,0:T(8,128)(2,1)} async-done(((bf16[1,300,1875]{2,1,0:T(8,128)(2,1)}), bf16[8,300,1875]{2,1,0:T(8,128)(2,1)}) %all-gather.3.cloned.1.call-update) | async-done | bytes 9000016 | tf_op jit(solution)/shard_map/all_gather | solution.py:41
  72.1 9.4 %reshape.21 = bf16[2400,1875]{1,0:T(8,128)(2,1)} reshape(bf16[8,300,1875]{2,1,0:T(8,128)(2,1)} %all-gather.3.cloned.1.call-done) | data formatting | bytes 18000000
  81.6 0.0 copy-done.2
  81.6 14.5 %fusion.1 = f32[2400,800]{1,0:T(8,128)} fusion(bf16[2400,1875]{1,0:T(8,128)(2,1)} %reshape.21, bf16[800,1875]{1,0:T(8,128)(2,1)S(1)} %copy-done.2, s32[1875]{0:T(1024)S(1)} %dynamic_slice.15, s32[800]{0:T(1024)S(1)} %dynamic_slice.19), kind=kOutput, calls=%fused_computation.1 | convolution fusion | flops 7202999808 | bytes 19690700 | tf_op jit(solution)/shard_map/dot_general | solution.py:15
  96.1 0.0 copy-start.1
  96.1 203.0 %fusion = f32[80,800]{1,0:T(8,128)S(1)} fusion(f32[2400,800]{1,0:T(8,128)} %fusion.1), kind=kCustom, calls=%all-reduce-scatter | all-reduce-scatter fusion | flops 2048001 | bytes 7937024
  299.2 1.9 collective-permute-start
  301.1 2.0 collective-permute-start.1
  303.2 0.0 copy-done.1
  303.2 0.6 dynamic-slice.4
  304.4 10.0 %collective-permute-done.1 = bf16[75,800]{1,0:T(8,128)(2,1)S(1)} collective-permute-done((bf16[75,800]{1,0:T(8,128)(2,1)S(1)}, bf16[75,800]{1,0:T(8,128)(2,1)S(1)}, u32[]{:S(2)}, u32[]{:S(2)}) %collective-permute-start.1) | collective-permute-done | bytes 120032
  314.4 0.0 collective-permute-done
  314.4 0.8 concatenate
  315.1 0.7 dynamic-slice_convert_fusion
  (2 shorter events, 0.0 us)
Async XLA Ops:
  6.5 7.7 %copy-start = (s32[100]{0:T(128)S(1)}, s32[100]{0:T(128)}, u32[]{:S(2)}) copy-start(s32[100]{0:T(128)} %param.9) | copy-start | bytes 1204
  6.5 65.6 %all-gather.3.cloned.1.call-start = ((), (), s32[]{:S(2)}) async-start(), calls=%async_computation | async-start | bytes 10506240 | tf_op jit(solution)/shard_map/all_gather | solution.py:41
  14.5 67.0 %copy-start.2 = (bf16[800,1875]{1,0:T(8,128)(2,1)S(1)}, bf16[800,1875]{1,0:T(8,128)(2,1)}, u32[]{:S(2)}) copy-start(bf16[800,1875]{1,0:T(8,128)(2,1)} %param.6) | copy-start | bytes 9000004
  96.1 207.1 %copy-start.1 = (u32[256]{0:T(256)S(1)}, u32[256]{0:T(256)}, u32[]{:S(2)}) copy-start(u32[256]{0:T(256)} %constant.38) | copy-start | bytes 3076
  299.2 15.2 %collective-permute-start = (bf16[80,800]{1,0:T(8,128)(2,1)S(1)}, bf16[80,800]{1,0:T(8,128)(2,1)S(1)}, u32[]{:S(2)}, u32[]{:S(2)}) collective-permute-start(bf16[80,800]{1,0:T(8,128)(2,1)S(1)} %convert), channel_id=1, source_target_pairs={{0,1},{1,2},{2,3},{3,4},{4,5},{5,6},{6,7},{7,8},{8,9},{9,10},{10,1... | collective-permute-start | bytes 384008
  301.1 13.2 %collective-permute-start.1 = (bf16[75,800]{1,0:T(8,128)(2,1)S(1)}, bf16[75,800]{1,0:T(8,128)(2,1)S(1)}, u32[]{:S(2)}, u32[]{:S(2)}) collective-permute-start(bf16[75,800]{1,0:T(8,128)(2,1)S(1)} %slice), channel_id=1, source_target_pairs={{0,2},{1,3},{2,4},{3,5},{4,6},{5,7},{6,8},{7,9},{8,10},{9,11},{10,... | collective-permute-start | bytes 360008
Sparse Core Ops, SparseCore 0:
  13.0 59.1 all-gather.2
where the time goes:
time: 323 us
  blocking collectives  203 us (63%)
  waiting for transfers between devices  67.6 us (21%)
  between operations  15.5 us (5%)
  matrix products  14.5 us (4%)
  local copies, waits for them, and re-layouts  13.8 us (4%)
  other arithmetic  4.32 us (1%)
  starting transfers between devices  3.95 us (1%)
    unnamed x1, blocking collectives  203 us
    all_gather x1, waiting for transfers between devices, body(): whole_columns = lax.all_gather(masked_integrals, 'row', axis=1, tiled=True)  57.6 us
    dot_general x1, matrix products, cycle_rows(): lax.dot_general(columns, masked_amplitudes, (((0,), (1,)), ((), ())), pre...  14.5 us
    unnamed x10, local copies, waits for them, and re-layouts  10.8 us
    unnamed x3, waiting for transfers between devices  9.97 us
  transfers between devices with their start and end apart: 3, of which 2 were waited for; matrix products, arithmetic and copies ran while one was open for 1% of the time, Pallas kernels for 0%

commit v1 on v0

v1 whole, which is shorter than its diff:
```python
import functools

import jax
import jax.numpy as jnp
from jax import lax
from jax.experimental import pallas as pl
from jax.experimental.pallas import tpu as pltpu
from jax.sharding import PartitionSpec as P

O = 100
VA = 64
VB = 24
PAIRS = 1875
PAIRS_PAD = 1920
ROWS = 800
COLUMNS = 300
OUT = 75
OUT_PAD = 80
SLOTS = 127
SLOT_LANES = 128
PACK = 64
F32 = jnp.float32
BF16 = jnp.bfloat16
I32 = jnp.int32
STEPS = 256.0
VMEM_LIMIT = 40 * 1024 * 1024


def iota(shape, dim):
    return lax.broadcasted_iota(I32, shape, dim)


def tenth(t):
    return (t * 5243) >> 19


def table_row(values):
    lane = iota((1, 128), 1)
    row = jnp.zeros((1, 128), I32)
    for at, value in enumerate(values):
        row = jnp.where(lane == at, value, row)
    return row


def occupied_values(occupied):
    return [occupied[k] for k in range(O)]


def virtual_values(virtual, start, count):
    return [virtual[jnp.minimum(start + n, 599)] for n in range(count)]


def lane_labels(occupied_row, virtual_row, k, c):
    n = k.shape[1]
    table = jnp.concatenate([occupied_row, virtual_row], axis=1).astype(F32)
    lane = iota((16, 256), 1)
    sub = iota((16, 256), 0)
    keep = ((sub == 0) & (lane < 128)) | ((sub == 1) & (lane >= 128))
    left = jnp.where(keep, jnp.broadcast_to(table, (16, 256)), 0.0).astype(BF16)
    place = iota((128, n), 0)
    right = jnp.concatenate(
        [jnp.where(place == k, 1.0, 0.0), jnp.where(place == c, 1.0, 0.0)], axis=0
    ).astype(BF16)
    both = jnp.dot(left, right, preferred_element_type=F32).astype(I32)
    return both[0:1] ^ both[1:2]


def column_labels(occupied_row, virtual_row, k, c):
    n = k.shape[0]
    lane = iota((n, 128), 1)
    left = jnp.concatenate(
        [jnp.where(lane == k, 1.0, 0.0), jnp.where(lane == c, 1.0, 0.0)], axis=1
    ).astype(BF16)
    occupied_column = jnp.transpose(jnp.broadcast_to(occupied_row, (128, 128)).astype(F32))
    virtual_column = jnp.transpose(jnp.broadcast_to(virtual_row, (128, 128)).astype(F32))
    zero = jnp.zeros((128, 128), F32)
    right = jnp.concatenate(
        [
            jnp.concatenate([occupied_column, zero], axis=1),
            jnp.concatenate([zero, virtual_column], axis=1),
        ],
        axis=0,
    ).astype(BF16)
    both = jnp.dot(left, right, preferred_element_type=F32).astype(I32)
    return both[:, :128] ^ both[:, 128:]


def pair_places(pair_block):
    base = pair_block * PAIRS
    first = lax.div(base, O)
    t = iota((1, PAIRS_PAD), 1) + (base - first * O)
    c = tenth(t)
    return first, t - c * O, c


def lane_rank(label):
    n = label.shape[1]
    same = iota((16, n), 0) == label
    earlier = jnp.where(iota((n, n), 0) < iota((n, n), 1), 1.0, 0.0).astype(BF16)
    counts = jnp.dot(jnp.where(same, 1.0, 0.0).astype(BF16), earlier, preferred_element_type=F32)
    return jnp.sum(jnp.where(same, counts, 0.0), axis=0, keepdims=True).astype(I32)


def pack_columns_kernel(virtual, occupied, starts, integrals, packed):
    row_block, pair_block, column_start, wpass = starts[0], starts[1], starts[3], starts[5]
    occupied_row = table_row(occupied_values(occupied))
    first, k_pair, c_pair = pair_places(pair_block)
    virtual_row = table_row(
        virtual_values(virtual, first, 20)
        + virtual_values(virtual, column_start + row_block * (COLUMNS // O), COLUMNS // O)
    )
    t = iota((1, 384), 1)
    c = tenth(t)
    label = lane_labels(
        occupied_row,
        virtual_row,
        jnp.concatenate([k_pair, t - c * O], axis=1),
        jnp.concatenate([c_pair, c + 20], axis=1),
    )
    label_pair = label[:, :PAIRS_PAD]
    label_column = jnp.where(t < COLUMNS, label[:, PAIRS_PAD:], -1)
    rank = lane_rank(label_column) - wpass * PACK
    key = jnp.where((rank >= 0) & (rank < PACK) & (t < COLUMNS), label_column * PACK + rank, -1)
    chosen = jnp.where(iota((8 * PACK, 384), 0) == key, 1.0, 0.0).astype(BF16)[:, :COLUMNS]
    moved = lax.dot_general(
        chosen, integrals[...], (((1,), (1,)), ((), ())), preferred_element_type=F32
    )
    total = jnp.zeros((PACK, PAIRS), F32)
    here = label_pair[:, :PAIRS]
    for g in range(8):
        total = jnp.where(here == g, moved[g * PACK : (g + 1) * PACK], total)
    packed[...] = jnp.zeros((PACK, PAIRS_PAD), BF16)
    packed[:, :PAIRS] = total.astype(BF16)


def pack_rows_kernel(
    virtual, occupied, starts, amplitudes, rows_packed, unpack, column_label, pair_label, row_places, staged
):
    row_block, pair_block, row_start, column_start = starts[0], starts[1], starts[2], starts[3]
    spass, wpass = starts[4], starts[5]
    occupied_row = table_row(occupied_values(occupied))
    first, k_pair, c_pair = pair_places(pair_block)
    virtual_row = table_row(
        virtual_values(virtual, first, 20)
        + virtual_values(virtual, row_start + row_block * (ROWS // O), ROWS // O)
    )
    t = iota((1, 896), 1)
    c = tenth(t)
    label = lane_labels(
        occupied_row,
        virtual_row,
        jnp.concatenate([k_pair, t - c * O], axis=1),
        jnp.concatenate([c_pair, c + 20], axis=1),
    )
    label_pair = label[:, :PAIRS_PAD]
    label_row = jnp.where(t < ROWS, label[:, PAIRS_PAD:], -1)
    rank = lane_rank(label_row) - spass * SLOTS
    taken = (rank >= 0) & (rank < SLOTS) & (t < ROWS)
    slot = jnp.where(taken, rank, -1)
    row_places[...] = jnp.where(
        iota((8, 896), 0) == 0, slot, jnp.where(iota((8, 896), 0) == 1, label_row, 0)
    )
    pair_bf16 = jnp.broadcast_to(label_pair, (16, PAIRS_PAD)).astype(F32).astype(BF16)
    pair_label[...] = pair_bf16

    p = iota((ROWS, 128), 0)
    a = tenth(p)
    row_column = column_labels(occupied_row, virtual_row, p - a * O, a + 20)
    row_column = row_column.astype(F32).astype(BF16)
    wide = jnp.concatenate([row_column] * (PAIRS_PAD // 128), axis=1)[:, :PAIRS]
    masked = jnp.where(wide == pair_bf16[0:1, :PAIRS], amplitudes[...], jnp.zeros((), BF16))
    chosen = jnp.where(iota((SLOT_LANES, 896), 0) == slot, 1.0, 0.0).astype(BF16)[:, :ROWS]
    staged[...] = jnp.zeros((SLOT_LANES, PAIRS_PAD), F32)
    staged[:, :PAIRS] = jnp.dot(chosen, masked, preferred_element_type=F32)
    rows_packed[...] = jnp.transpose(staged[...]).astype(BF16)

    window = table_row(virtual_values(virtual, column_start, VB))
    x, core = lax.div(row_block, 2), lax.rem(row_block, 2)
    e = iota((OUT_PAD, 128), 0)
    lane = iota((4 * OUT_PAD, 128), 1)
    earlier = jnp.where(
        iota((4 * OUT_PAD, 4 * OUT_PAD), 1) < iota((4 * OUT_PAD, 4 * OUT_PAD), 0), 1.0, 0.0
    ).astype(BF16)
    for step in range(4):
        for half in range(2):
            shard = lax.rem(x - step + 4, 4) * 2 + half
            t = jnp.concatenate([e + d * OUT for d in range(4)], axis=0)
            valid = jnp.concatenate([e] * 4, axis=0) < OUT
            b = tenth(t)
            labels = column_labels(occupied_row, window, t - b * O, b + shard * (COLUMNS // O))
            labels = jnp.where(valid, labels, -1)
            same = labels == lane
            counts = jnp.dot(earlier, jnp.where(same, 1.0, 0.0).astype(BF16), preferred_element_type=F32)
            rank = jnp.sum(jnp.where(same, counts, 0.0), axis=1, keepdims=True).astype(I32) - wpass * PACK
            at = jnp.where((rank >= 0) & (rank < PACK), rank + PACK * jnp.bitwise_xor(core, half), -1)
            mine = jnp.where(valid & (lane == at), 1.0, 0.0).astype(BF16)
            rows = pl.ds((step * 2 + half) * 4 * OUT_PAD, 4 * OUT_PAD)
            unpack[rows, :] = mine
            column_label[rows, :] = labels.astype(F32).astype(BF16)


def contract_kernel(starts, unpack, column_label, pair_label, rows_packed, *refs):
    shards, sums = refs[:8], refs[8]
    x = lax.div(starts[0], 2)
    rows = rows_packed[...]
    here = pair_label[...][0:1]
    n = 4 * OUT_PAD
    lane = iota((n, SLOT_LANES), 1)
    for step in range(4):
        pair = jnp.concatenate([shards[2 * step][...], shards[2 * step + 1][...]], axis=0)
        for half in range(2):
            at = pl.ds((step * 2 + half) * n, n)
            spread = jnp.dot(unpack[at, :], pair, preferred_element_type=F32).astype(BF16)
            wide = jnp.concatenate([column_label[at, :]] * (PAIRS_PAD // 128), axis=1)
            masked = jnp.where(wide == here, spread, jnp.zeros((), BF16))
            part = jnp.dot(masked, rows, preferred_element_type=F32)
            top = jnp.max(jnp.abs(part), axis=1, keepdims=True)
            exponent = jnp.ceil(jnp.log2(jnp.maximum(top, 2.0**-120)) * STEPS)
            back = jnp.exp2(15.0 - exponent * (1.0 / STEPS))
            coded = jnp.clip(jnp.round(part * back), -32767.0, 32767.0)
            coded = jnp.where(lane == SLOTS, exponent, coded).astype(I32).astype(jnp.int16)
            shard = lax.rem(x - step + 4, 4) * 2 + half
            for d in range(4):
                sums[shard * 4 + d] = coded[d * OUT_PAD : (d + 1) * OUT_PAD]


def spread_kernel(virtual, occupied, starts, row_places, parts, out):
    column_start, place = starts[3], starts[6]
    occupied_row = table_row(occupied_values(occupied))
    first = lax.div(place * OUT, O)
    virtual_row = table_row(virtual_values(virtual, column_start + first, 2))
    t = iota((OUT_PAD, 128), 0) + (place * OUT - first * O)
    c = tenth(t)
    labels = column_labels(occupied_row, virtual_row, t - c * O, c)
    labels = labels.astype(F32)
    total = jnp.zeros((OUT_PAD, SLOT_LANES), F32)
    for d in range(parts.shape[0]):
        part = parts[d].astype(I32).astype(F32)
        total = total + part * jnp.exp2(part[:, SLOTS:] * (1.0 / STEPS) - 15.0)
    lane = iota((OUT_PAD, SLOT_LANES), 1)
    total = jnp.where(lane < SLOTS, total, 0.0).astype(BF16)
    slot = row_places[0:1, :]
    label_row = row_places[1:2, :].astype(F32)
    chosen = jnp.where(iota((SLOT_LANES, 896), 0) == slot, 1.0, 0.0).astype(BF16)
    spread = jnp.dot(total, chosen, preferred_element_type=F32)
    wide = jnp.concatenate([labels] * 7, axis=1)
    spread = jnp.where(wide == label_row, spread, 0.0).astype(BF16)
    out[...] = spread[:OUT, :ROWS]


SMEM = pl.BlockSpec(memory_space=pltpu.SMEM)
VMEM = pl.BlockSpec(memory_space=pltpu.VMEM)


def call(kernel, name, ins, outs, scratch=(), flops=0, moved=0):
    return pl.pallas_call(
        kernel,
        name=name,
        in_specs=ins,
        out_specs=[VMEM] * len(outs) if len(outs) > 1 else VMEM,
        out_shape=outs if len(outs) > 1 else outs[0],
        scratch_shapes=scratch,
        compiler_params=pltpu.CompilerParams(vmem_limit_bytes=VMEM_LIMIT),
        cost_estimate=pl.CostEstimate(flops=flops, bytes_accessed=moved, transcendentals=0),
    )


def shape(dims, kind):
    return jax.ShapeDtypeStruct(dims, kind)


def one_pass(amplitudes, integrals, virtual_irrep, occupied_irrep, starts):
    packed = call(
        pack_columns_kernel,
        "pack_columns",
        [SMEM, SMEM, SMEM, VMEM],
        [shape((PACK, PAIRS_PAD), BF16)],
        flops=2 * 8 * PACK * COLUMNS * PAIRS,
        moved=2 * PAIRS * (COLUMNS + PACK),
    )(virtual_irrep, occupied_irrep, starts, integrals)
    sibling = [(i, i ^ 1) for i in range(8)]
    own = [packed]
    for step in range(1, 4):
        own.append(lax.ppermute(packed, "row", [(i, (i + 2 * step) % 8) for i in range(8)]))
    other = [lax.ppermute(block, "row", sibling) for block in own]
    shards = [block for pair in zip(own, other) for block in pair]
    rows_packed, unpack, column_label, pair_label, row_places = call(
        pack_rows_kernel,
        "pack_rows",
        [SMEM, SMEM, SMEM, VMEM],
        [
            shape((PAIRS_PAD, SLOT_LANES), BF16),
            shape((8 * 4 * OUT_PAD, 128), BF16),
            shape((8 * 4 * OUT_PAD, 128), BF16),
            shape((16, PAIRS_PAD), BF16),
            shape((8, 896), I32),
        ],
        [pltpu.VMEM((SLOT_LANES, PAIRS_PAD), F32)],
        flops=8 * 2 * SLOT_LANES * ROWS * PAIRS,
        moved=2 * PAIRS * ROWS * 3,
    )(virtual_irrep, occupied_irrep, starts, amplitudes)
    sums = call(
        contract_kernel,
        "contract",
        [SMEM] + [VMEM] * 12,
        [shape((32, OUT_PAD, SLOT_LANES), jnp.int16)],
        flops=2 * 2400 * PAIRS_PAD * 256,
        moved=2 * 8 * PACK * PAIRS_PAD,
    )(starts, unpack, column_label, pair_label, rows_packed, *shards)
    parts = lax.all_to_all(sums, ("col", "depth"), 0, 0)
    return call(
        spread_kernel,
        "spread",
        [SMEM, SMEM, SMEM, VMEM, VMEM],
        [shape((OUT, ROWS), BF16)],
        flops=2 * OUT * ROWS * 128,
        moved=2 * 32 * OUT_PAD * SLOT_LANES,
    )(virtual_irrep, occupied_irrep, starts, row_places, parts)


def most(labels):
    return jnp.max(jnp.sum((labels[:, None, :] == jnp.arange(8)[None, :, None]).astype(I32), axis=2))


def body(amplitudes, integrals, virtual_irrep, occupied_irrep, row_start, column_start):
    row_block = lax.axis_index("row").astype(I32)
    pair_block = lax.axis_index(("col", "depth")).astype(I32)

    def starts(spass, wpass):
        return jnp.stack(
            [
                row_block,
                pair_block,
                row_start[0],
                column_start[0],
                jnp.asarray(spass, I32),
                jnp.asarray(wpass, I32),
                pair_block,
                jnp.zeros((), I32),
            ]
        )

    run = functools.partial(one_pass, amplitudes, integrals, virtual_irrep, occupied_irrep)
    first = run(starts(0, 0))

    def labels_of(start, count, blocks):
        part = lax.dynamic_slice_in_dim(virtual_irrep, start[0], count)
        return jnp.bitwise_xor(
            part.reshape(blocks, count // blocks, 1), occupied_irrep[None, None, :]
        ).reshape(blocks, -1)

    spasses = lax.div(most(labels_of(row_start, VA, 8)) + (SLOTS - 1), SLOTS)
    wpasses = lax.div(most(labels_of(column_start, VB, 8)) + (PACK - 1), PACK)
    passes = spasses * wpasses

    def more(state):
        return state[0] < passes

    def again(state):
        at, out = state
        wpass = lax.rem(at, wpasses)
        return at + 1, out + run(starts(lax.div(at, wpasses), wpass))

    return lax.while_loop(more, again, (jnp.ones((), I32), first))[1]


def solution(mesh):
    return jax.shard_map(
        body,
        mesh=mesh,
        in_specs=(P("row", ("col", "depth")), P(("col", "depth"), "row"), P(), P(), P(), P()),
        out_specs=P(("col", "depth"), "row"),
        check_vma=False,
    )
```

time: 323 us -> 71.4 us (0.22)
  the two profiles are of different devices: /device:TPU:8 before, /device:TPU:1 now
where the time goes in v1:
time: 71.4 us; the launch traced here: 71.1 us
  waiting for transfers between devices  24.7 us (35%)
  starting transfers between devices  21.7 us (30%)
  Pallas kernels  16.4 us (23%)
  local copies, waits for them, and re-layouts  3.8 us (5%)
  between operations  2.76 us (4%)
  other arithmetic  1.77 us (2%)
    all_to_all x1, waiting for transfers between devices, one_pass(): parts = lax.all_to_all(sums, ('col', 'depth'), 0, 0)  16.6 us
    all_to_all x1, starting transfers between devices, one_pass(): parts = lax.all_to_all(sums, ('col', 'depth'), 0, 0)  11.2 us
    ppermute x3, waiting for transfers between devices, one_pass(): lax.ppermute(packed, 'row', [(i, (i + 2 * step) % 8) for i in range(8)])  8.08 us
    pallas_call x1, Pallas kernels, one_pass(): call(contract_kernel, 'contract', [SMEM] + [VMEM] * 12, [shape((32, OUT_P...  6.88 us
    pallas_call x1, Pallas kernels, one_pass(): call(pack_rows_kernel, 'pack_rows', [SMEM, SMEM, SMEM, VMEM], [shape((PAI...  5.97 us
    ppermute x4, starting transfers between devices, one_pass(): other = [lax.ppermute(block, 'row', sibling) for block in own]  5.94 us
    ppermute x3, starting transfers between devices, one_pass(): lax.ppermute(packed, 'row', [(i, (i + 2 * step) % 8) for i in range(8)])  4.51 us
    unnamed x7, local copies, waits for them, and re-layouts  2.94 us
  transfers between devices with their start and end apart: 8, of which 3 were waited for; matrix products, arithmetic and copies ran while one was open for 4% of the time, Pallas kernels for 8%

profile of v1, /device:TPU:1, one launch (start us, length us, event | category | flops | bytes accessed | tf_op | source)
XLA Modules:
  0.0 71.1 jit_solution(18201020913934829229)
XLA Ops:
  1.3 2.3 %copy.11.integrals = bf16[1875,300]{1,0:T(8,128)(2,1)S(1)} copy(bf16[1875,300]{0,1:T(8,128)(2,1)} %param.9) | data formatting | bytes 2250000 | tf_op args[1]
  3.6 0.1 stack.28.starts
  3.7 2.3 %pack_columns.2.refs_0_ = bf16[64,1920]{1,0:T(8,128)(2,1)S(1)} custom-call(s32[600]{0:T(1024)S(1)} %copy-done.1, s32[100]{0:T(128)S(1)} %copy-done.2, s32[8]{0:T(128)S(1)} %stack.28.starts, bf16[1875,300]{1,0:T(8,128)(2,1)S(1)} %copy.11.integrals), custom_call_target="tpu_custom_call" | custom-call | flops 576000000 | bytes 1365000 | tf_op jit(solution)/shard_map/pack_columns/pallas_call | solution.py:273
  6.1 3.4 %collective-permute-start.12 = (bf16[64,1920]{1,0:T(8,128)(2,1)S(1)}, bf16[64,1920]{1,0:T(8,128)(2,1)S(1)}, u32[]{:S(2)}, u32[]{:S(2)}) collective-permute-start(bf16[64,1920]{1,0:T(8,128)(2,1)S(1)} %pack_columns.2.refs_0_), channel_id=1, source_target_pairs={{0,192},{32,224},{64,0},{96,32},{128,64},{160,96},{192,128},{224,1... | collective-permute-start | bytes 737288 | tf_op jit(solution)/shard_map/ppermute | solution.py:284
  9.5 0.5 collective-permute-start.10
  10.0 0.6 collective-permute-start.8
  10.6 1.5 %collective-permute-start.7 = (bf16[64,1920]{1,0:T(8,128)(2,1)S(1)}, bf16[64,1920]{1,0:T(8,128)(2,1)S(1)}, u32[]{:S(2)}, u32[]{:S(2)}) collective-permute-start(bf16[64,1920]{1,0:T(8,128)(2,1)S(1)} %pack_columns.2.refs_0_), channel_id=1, source_target_pairs={{0,32},{32,0},{64,96},{96,64},{128,160},{160,128},{192,224},{224,1... | collective-permute-start | bytes 737288 | tf_op jit(solution)/shard_map/ppermute | solution.py:285
  12.1 4.9 %collective-permute-done.12.refs_6_ = bf16[64,1920]{1,0:T(8,128)(2,1)S(1)} collective-permute-done((bf16[64,1920]{1,0:T(8,128)(2,1)S(1)}, bf16[64,1920]{1,0:T(8,128)(2,1)S(1)}, u32[]{:S(2)}, u32[]{:S(2)}) %collective-permute-start.12) | collective-permute-done | bytes 245792 | tf_op jit(solution)/shard_map/ppermute | solution.py:284
  17.0 3.9 %collective-permute-start.13 = (bf16[64,1920]{1,0:T(8,128)(2,1)S(1)}, bf16[64,1920]{1,0:T(8,128)(2,1)S(1)}, u32[]{:S(2)}, u32[]{:S(2)}) collective-permute-start(bf16[64,1920]{1,0:T(8,128)(2,1)S(1)} %collective-permute-done.12.refs_6_), channel_id=1, source_target_pairs={{0,32},{32,0},{64,96},{96,64},{128,160},{160,128},{192,224},{224,1... | collective-permute-start | bytes 737288 | tf_op jit(solution)/shard_map/ppermute | solution.py:285
  20.9 3.2 %collective-permute-done.8.refs_2_ = bf16[64,1920]{1,0:T(8,128)(2,1)S(1)} collective-permute-done((bf16[64,1920]{1,0:T(8,128)(2,1)S(1)}, bf16[64,1920]{1,0:T(8,128)(2,1)S(1)}, u32[]{:S(2)}, u32[]{:S(2)}) %collective-permute-start.8) | collective-permute-done | bytes 245792 | tf_op jit(solution)/shard_map/ppermute | solution.py:284
  24.1 0.5 collective-permute-start.9
  24.6 6.0 %pack_rows.2 = (bf16[1920,128]{1,0:T(8,128)(2,1)S(1)}, bf16[2560,128]{1,0:T(8,128)(2,1)S(1)}, bf16[2560,128]{1,0:T(8,128)(2,1)S(1)}, bf16[16,1920]{1,0:T(8,128)(2,1)S(1)}, s32[8,896]{1,0:T(8,128)S(1)}) custom-call(s32[600]{0:T(1024)S(1)} %copy-done.1, s32[100]{0:T(128)S(1)} %copy-done.2, s32[8]{0:T(128)S(1)} %stack.28.starts, bf16[800,1875]{1,0:T(8,128)(2,1)} %amplitudes.1), custom_call_target="tpu_custom_call" | custom-call | flops 3072000000 | bytes 9000000 | tf_op jit(solution)/shard_map/pack_rows/pallas_call | solution.py:287
  30.6 6.9 %contract.2 = s16[32,80,128]{2,1,0:T(8,128)(2,1)} custom-call(s32[8]{0:T(128)S(1)} %stack.28.starts, bf16[2560,128]{1,0:T(8,128)(2,1)S(1)} %get-tuple-element.79.unpack, bf16[2560,128]{1,0:T(8,128)(2,1)S(1)} %get-tuple-element.80.column_label, bf16[16,1920]{1,0:T(8,128)(2,1)S(1)} %get-tuple-element.81.pair_label, ...), custom_call_target="tpu_custom_call" | custom-call | flops 2359296000 | bytes 1966080 | tf_op jit(solution)/shard_map/contract/pallas_call | solution.py:302
  37.5 11.2 %all-to-all-start.1 = ((s16[32,80,128]{2,1,0:T(8,128)(2,1)}), s16[32,80,128]{2,1,0:T(8,128)(2,1)S(1)}, u32[]{:S(2)}, u32[]{:S(2)}) async-start(s16[32,80,128]{2,1,0:T(8,128)(2,1)} %contract.2), calls=%async_computation.1 | async-start | bytes 1310720 | tf_op jit(solution)/shard_map/all_to_all | solution.py:310
  48.7 0.1 dynamic_slice.7
  48.8 0.1 xor.61
  48.9 0.1 xor.57
  49.0 0.1 xor.58
  49.0 0.1 xor.59
  49.1 0.2 convert_reduce_fusion.1
  49.4 0.6 reduce_max.19
  50.7 0.1 dynamic_slice.6
  50.7 0.1 xor.50
  50.8 0.1 xor.54
  50.9 0.1 xor.51
  51.0 0.1 xor.52
  51.1 0.2 convert_reduce_fusion
  51.3 0.7 reduce_max.18
  52.6 16.6 %all-to-all-done.1.parts = s16[32,80,128]{2,1,0:T(8,128)(2,1)S(1)} async-done(((s16[32,80,128]{2,1,0:T(8,128)(2,1)}), s16[32,80,128]{2,1,0:T(8,128)(2,1)S(1)}, u32[]{:S(2)}, u32[]{:S(2)}) %all-to-all-start.1) | async-done | bytes 655392 | tf_op jit(solution)/shard_map/all_to_all | solution.py:310
  69.2 1.2 %spread.2 = bf16[75,800]{1,0:T(8,128)(2,1)S(1)} custom-call(s32[600]{0:T(1024)S(1)} %copy-done.1, s32[100]{0:T(128)S(1)} %copy-done.2, s32[8]{0:T(128)S(1)} %stack.28.starts, s32[8,896]{1,0:T(8,128)S(1)} %get-tuple-element.78.row_places, s16[32,80,128]{2,1,0:T(8,128)(2,1)S(1)} %all-to-all-done.1.parts), custom_call_target="tpu_custom_call" | custom-call | flops 15360000 | bytes 655360 | tf_op jit(solution)/shard_map/spread/pallas_call | solution.py:311
  70.4 0.0 copy-start
  70.5 0.7 copy-done
  (16 shorter events, 0.1 us)
Async XLA Ops:
  0.0 3.7 %copy-start.2 = (s32[100]{0:T(128)S(1)}, s32[100]{0:T(128)}, u32[]{:S(2)}) copy-start(s32[100]{0:T(128)} %occupied.5) | copy-start | bytes 1204
  0.0 3.7 %copy-start.1 = (s32[600]{0:T(1024)S(1)}, s32[600]{0:T(1024)}, u32[]{:S(2)}) copy-start(s32[600]{0:T(1024)} %virtual.5) | copy-start | bytes 7204
  6.1 10.9 %collective-permute-start.12 = (bf16[64,1920]{1,0:T(8,128)(2,1)S(1)}, bf16[64,1920]{1,0:T(8,128)(2,1)S(1)}, u32[]{:S(2)}, u32[]{:S(2)}) collective-permute-start(bf16[64,1920]{1,0:T(8,128)(2,1)S(1)} %pack_columns.2.refs_0_), channel_id=1, source_target_pairs={{0,192},{32,224},{64,0},{96,32},{128,64},{160,96},{192,128},{224,1... | collective-permute-start | bytes 737288 | tf_op jit(solution)/shard_map/ppermute | solution.py:284
  9.5 11.4 %collective-permute-start.10 = (bf16[64,1920]{1,0:T(8,128)(2,1)S(1)}, bf16[64,1920]{1,0:T(8,128)(2,1)S(1)}, u32[]{:S(2)}, u32[]{:S(2)}) collective-permute-start(bf16[64,1920]{1,0:T(8,128)(2,1)S(1)} %pack_columns.2.refs_0_), channel_id=1, source_target_pairs={{0,128},{32,160},{64,192},{96,224},{128,0},{160,32},{192,64},{224,... | collective-permute-start | bytes 737288 | tf_op jit(solution)/shard_map/ppermute | solution.py:284
  10.0 14.1 %collective-permute-start.8 = (bf16[64,1920]{1,0:T(8,128)(2,1)S(1)}, bf16[64,1920]{1,0:T(8,128)(2,1)S(1)}, u32[]{:S(2)}, u32[]{:S(2)}) collective-permute-start(bf16[64,1920]{1,0:T(8,128)(2,1)S(1)} %pack_columns.2.refs_0_), channel_id=1, source_target_pairs={{0,64},{32,96},{64,128},{96,160},{128,192},{160,224},{192,0},{224,... | collective-permute-start | bytes 737288 | tf_op jit(solution)/shard_map/ppermute | solution.py:284
  10.6 20.0 %collective-permute-start.7 = (bf16[64,1920]{1,0:T(8,128)(2,1)S(1)}, bf16[64,1920]{1,0:T(8,128)(2,1)S(1)}, u32[]{:S(2)}, u32[]{:S(2)}) collective-permute-start(bf16[64,1920]{1,0:T(8,128)(2,1)S(1)} %pack_columns.2.refs_0_), channel_id=1, source_target_pairs={{0,32},{32,0},{64,96},{96,64},{128,160},{160,128},{192,224},{224,1... | collective-permute-start | bytes 737288 | tf_op jit(solution)/shard_map/ppermute | solution.py:285
  17.0 13.6 %collective-permute-start.13 = (bf16[64,1920]{1,0:T(8,128)(2,1)S(1)}, bf16[64,1920]{1,0:T(8,128)(2,1)S(1)}, u32[]{:S(2)}, u32[]{:S(2)}) collective-permute-start(bf16[64,1920]{1,0:T(8,128)(2,1)S(1)} %collective-permute-done.12.refs_6_), channel_id=1, source_target_pairs={{0,32},{32,0},{64,96},{96,64},{128,160},{160,128},{192,224},{224,1... | collective-permute-start | bytes 737288 | tf_op jit(solution)/shard_map/ppermute | solution.py:285
  20.9 9.7 %collective-permute-start.11 = (bf16[64,1920]{1,0:T(8,128)(2,1)S(1)}, bf16[64,1920]{1,0:T(8,128)(2,1)S(1)}, u32[]{:S(2)}, u32[]{:S(2)}) collective-permute-start(bf16[64,1920]{1,0:T(8,128)(2,1)S(1)} %collective-permute-done.10.refs_4_), channel_id=1, source_target_pairs={{0,32},{32,0},{64,96},{96,64},{128,160},{160,128},{192,224},{224,1... | collective-permute-start | bytes 737288 | tf_op jit(solution)/shard_map/ppermute | solution.py:285
  24.1 6.5 %collective-permute-start.9 = (bf16[64,1920]{1,0:T(8,128)(2,1)S(1)}, bf16[64,1920]{1,0:T(8,128)(2,1)S(1)}, u32[]{:S(2)}, u32[]{:S(2)}) collective-permute-start(bf16[64,1920]{1,0:T(8,128)(2,1)S(1)} %collective-permute-done.8.refs_2_), channel_id=1, source_target_pairs={{0,32},{32,0},{64,96},{96,64},{128,160},{160,128},{192,224},{224,1... | collective-permute-start | bytes 737288 | tf_op jit(solution)/shard_map/ppermute | solution.py:285
  37.5 31.7 %all-to-all-start.1 = ((s16[32,80,128]{2,1,0:T(8,128)(2,1)}), s16[32,80,128]{2,1,0:T(8,128)(2,1)S(1)}, u32[]{:S(2)}, u32[]{:S(2)}) async-start(s16[32,80,128]{2,1,0:T(8,128)(2,1)} %contract.2), calls=%async_computation.1 | async-start | bytes 1310720 | tf_op jit(solution)/shard_map/all_to_all | solution.py:310
  70.4 0.7 copy-start
